TPU v7x, 128 devices: a whole 4x4x4 slice. The times are simulated.
128 devices in a mesh: row: 8 (over z, y_hi), col: 16 (over x, y_lo, core).
Axes of the slice: x: 4, y: 4 (y_hi: 2, y_lo: 2; y = y_hi * 2 + y_lo), z: 4, core: 2. Of those that a mesh axis runs over, the one named last changes fastest.
Arguments:
- val_wave: bfloat16 [8, 64, 64, 128], replicated, may hold values from -6 to 6
- cond_wave: bfloat16 [128, 64, 64, 128], P(('row', 'col')), may hold values from -6 to 6
- val_energy: float32 [8], replicated, may hold values from -12 to -0.5
- cond_energy: float32 [128], replicated, may hold values from 0.5 to 20
- band_owner: int32 [128], P(('row', 'col')), may hold values from 0 to 127, each once
- grid_map: int32 [30720], replicated, may hold values from 0 to 262143, as said below
Outputs:
- chi: float32 [2, 2048, 30720], P(None, 'row', 'col')
Inputs may be any that keep to these rules, and one draw needn't show every extreme that they name: `band_owner`: every one of the 128 band numbers stands in exactly one slot. `grid_map`: 30720 distinct flat grid points: those of the shortest wave vectors, with indices above 32 read as negative frequencies, ordered by length with ties in random order.
All inputs are finite; a program needn't handle non-finite values.
Results may differ from a plain program's by a relative error of at most 0.0041.
Values may be sent and summed in bfloat16 or wider, within the bound.
A program may use at most 576 MiB of HBM per device.

v0:
```python
import math

import jax
import jax.numpy as jnp
import ml_dtypes
import numpy as np
from jax import lax
from jax.experimental import pallas as pl
from jax.experimental.pallas import tpu as pltpu
from jax.sharding import PartitionSpec as P

GRID = 64
NG = 30720
SLAB = 2048
ROWS = 8
COLS = 16
G_COL = NG // COLS
G_ROW = SLAB // ROWS
MAGS = 20
CELLS = MAGS * MAGS
LANES = 128


def shells():
    points = np.arange(GRID)
    freq = np.where(points < GRID // 2, points, points - GRID)
    square = freq * freq
    length = (square[:, None, None] + square[None, :, None] + square[None, None, :]).ravel()
    length = np.sort(length, kind="stable")
    assert length[NG - 1] < MAGS * MAGS
    return length


def orbit_lists(width, count):
    length = shells()
    mags = np.arange(MAGS)
    a, b, c = np.meshgrid(mags, mags, mags, indexing="ij")
    a, b, c = a.ravel(), b.ravel(), c.ravel()
    square = a * a + b * b + c * c
    source = c * CELLS + (b // 4) * (4 * MAGS) + a * 4 + b % 4
    code = (a * GRID + b) * GRID + c
    order = np.argsort(square, kind="stable")
    lists = []
    for block in range(count):
        least, most = length[block * width], length[(block + 1) * width - 1]
        lists.append(order[(square[order] >= least) & (square[order] <= most)])
    rows = -(-max(len(picked) for picked in lists) // 16) * 16
    index = np.zeros((count, rows), np.int32)
    codes = np.full((count, 1, rows), -1, np.int32)
    for block, picked in enumerate(lists):
        index[block, : len(picked)] = source[picked]
        codes[block, 0, : len(picked)] = code[picked]
    return index, codes, [square[picked] for picked in lists]


def split_table(table):
    high = table.astype(ml_dtypes.bfloat16)
    low = (table - high.astype(np.float64)).astype(ml_dtypes.bfloat16)
    return np.concatenate([high, low], 0)


def dft_tables():
    point = np.arange(GRID)
    mag = np.arange(MAGS)
    angle = (mag[:, None] * point[None, :] % GRID) * (2.0 * math.pi / GRID)
    parts = np.stack([np.cos(angle), np.sin(angle)])
    table_b = np.zeros((2, MAGS // 4, 4, 4, 4, GRID))
    for a in range(4):
        table_b[:, :, a, :, a, :] = parts.reshape(2, MAGS // 4, 4, GRID)
    table_a = np.zeros((2, MAGS, 4, GRID, 4))
    for b in range(4):
        table_a[:, :, b, :, b] = parts
    table_c = np.zeros((MAGS, 2, 2, 2, 2, 2, GRID))
    for v in range(2):
        for sign in range(2):
            turn = 1.0 - 2.0 * sign
            table_c[:, v, 0, sign, 0, v] = parts[0]
            table_c[:, v, 0, sign, 1, v] = turn * parts[1]
            table_c[:, v, 1, sign, 1, v] = parts[0]
            table_c[:, v, 1, sign, 0, v] = -turn * parts[1]
    table_c = table_c * (1.0 / float(GRID) ** 1.5)
    return (
        split_table(table_b.reshape(8 * MAGS, 4 * GRID)),
        split_table(table_a.reshape(8 * MAGS, 4 * GRID)),
        split_table(table_c.reshape(8 * MAGS, 4 * GRID)),
    )


def dot_nn(left, right):
    return lax.dot_general(
        left, right, (((1,), (0,)), ((), ())), preferred_element_type=jnp.float32
    )


def dot_nt(left, right):
    return lax.dot_general(
        left, right, (((1,), (1,)), ((), ())), preferred_element_type=jnp.float32
    )


def halves(value):
    high = value.astype(jnp.bfloat16)
    return high, (value - high.astype(jnp.float32)).astype(jnp.bfloat16)


def three(dot, table, high, low):
    rows = table.shape[0] // 2
    both = dot(table, high)
    return both[:rows] + both[rows:] + dot(table[:rows], low)


def signs(both, rows):
    cos_re, cos_im = both[:rows, :LANES], both[:rows, LANES:]
    sin_re, sin_im = both[rows:, :LANES], both[rows:, LANES:]
    plus = jnp.concatenate([cos_re + sin_im, cos_im - sin_re], 1)
    minus = jnp.concatenate([cos_re - sin_im, cos_im + sin_re], 1)
    return plus, minus


def windows(width, count, tile):
    length = shells()
    _, codes, squares = orbit_lists(width, count)
    starts, ends = [], []
    for at in range(0, width, tile):
        first, last = [], []
        for block, square in enumerate(squares):
            first.append(np.searchsorted(square, length[block * width + at], "left"))
            last.append(np.searchsorted(square, length[block * width + at + tile - 1], "right"))
        starts.append(int(min(first)) // 32 * 16)
        ends.append(-(-int(max(last)) // 2))
    rows = max(-(-(end - start) // 16) * 16 for start, end in zip(starts, ends))
    return [min(start, codes.shape[2] // 2 - rows) for start in starts], rows


def paired(codes):
    return np.stack([codes[:, 0, 0::2], codes[:, 0, 1::2]], 1)


def fold_table(count, width):
    fold = np.zeros((count, LANES, width), ml_dtypes.bfloat16)
    lane = np.arange(LANES)
    for source in range(count):
        fold[source, lane, source * 8 + (lane >> 1) % 8] = 1.0
    return fold.reshape(count * LANES, width)


def turn_table():
    table = np.zeros((LANES, LANES), ml_dtypes.bfloat16)
    lane = np.arange(0, LANES, 2)
    table[lane + 1, lane] = 1.0
    table[lane, lane + 1] = -1.0
    return table


def placed(point, codes, slabs, fold):
    a, b, c = point >> 12, (point >> 6) & 63, point & 63
    half = GRID // 2
    code = (jnp.where(a > half, GRID - a, a) * GRID + jnp.where(b > half, GRID - b, b)) * GRID
    code = code + jnp.where(c > half, GRID - c, c)
    odd = jnp.where(code == codes[1:2], 1.0, 0.0)
    hot = jnp.where(code == codes[0:1], 1.0, odd).astype(jnp.bfloat16)
    key = (
        jnp.where(jnp.sum(odd, axis=1, keepdims=True) > 0.5, 8, 0)
        + jnp.where(a > half, 4, 0) + jnp.where(b > half, 2, 0) + jnp.where(c > half, 1, 0)
    )
    lane = lax.broadcasted_iota(jnp.int32, (1, 2 * LANES), 1) % LANES
    own = key == (lane >> 4) * 2 + lane % 2
    rows = []
    for pair in range(len(slabs) // 2):
        both = jnp.concatenate([slabs[2 * pair], slabs[2 * pair + 1]], 1)
        rows.append(jnp.where(own, dot_nn(hot, both), 0.0).astype(jnp.bfloat16))
    return dot_nn(jnp.concatenate(rows, 1), fold)


TILE = 384
TILES = G_COL // TILE
KINDS = 9


def whole_kernel(
    owner, cond_energy, val_energy, index_p, index_w,
    grid_map, codes_p, codes_w, table_b, table_a, table_c, fold_p, fold_w, turn, val_hbm, cond_hbm,
    out,
    val, cond, slots, zh, zl, uh, ul, sums, cells, picked, points_p, points_w, lines,
    plain, weighted, slabs, slabs_w, lefts, lefts_wide, left, panels, totals,
    val_sem, cond_sem, own_sem, out_sem,
    col_send, col_recv, row_send, row_recv, left_send, left_recv, move_send, move_recv,
):
    row, col = lax.axis_index("row"), lax.axis_index("col")
    z, y_hi = row // 2, lax.rem(row, 2)
    x, y_lo, core = col // 4, lax.rem(col // 2, 2), lax.rem(col, 2)
    up, down, far = lax.rem(z + 1, 4), lax.rem(z + 3, 4), lax.rem(z + 2, 4)
    above, below = (up * 2 + y_hi, col), (down * 2 + y_hi, col)
    across_row = z * 2 + 1 - y_hi
    across = (across_row, col)
    slot = core * 8 + col // 2
    mesh = pl.DeviceIdType.MESH

    fetch_cond = pltpu.make_async_copy(cond_hbm, cond, cond_sem)
    fetch_cond.start()
    fetch_val = []
    for pair in range(4):
        copy = pltpu.make_async_copy(val_hbm.at[pl.ds(2 * pair, 2)], val.at[pair], val_sem.at[pair])
        copy.start()
        fetch_val.append(copy)

    barrier = pltpu.get_barrier_semaphore()
    for i in range(1, COLS):
        pl.semaphore_signal(barrier, inc=1, device_id=(row, lax.rem(col + i, COLS)), device_id_type=mesh)
    for i in range(1, ROWS):
        pl.semaphore_signal(barrier, inc=1, device_id=(lax.rem(row + i, ROWS), col), device_id_type=mesh)

    lines[...] = jnp.zeros_like(lines)
    count_p, count_w = G_COL // LANES, G_ROW // LANES
    for i in range(count_p):
        lines[i : i + 1, :] = grid_map[pl.ds(col * count_p + i, 1), :].astype(jnp.float32)
    for i in range(count_w):
        lines[16 + i : 17 + i, :] = grid_map[pl.ds(row * count_w + i, 1), :].astype(jnp.float32)
    upright = jnp.transpose(lines[...], (1, 0)).astype(jnp.int32)
    for i in range(count_p):
        points_p[i * LANES : (i + 1) * LANES, :] = upright[:, i : i + 1]
    for i in range(count_w):
        points_w[i * LANES : (i + 1) * LANES, :] = upright[:, 16 + i : 17 + i]

    block = 4 * GRID
    first = lax.broadcasted_iota(jnp.int32, (block, LANES), 1) < GRID

    def widen(t, carry):
        slot_wave = cond[0, pl.ds(t * 4, 4)].reshape(block, LANES).astype(jnp.float32)
        turned = pltpu.roll(slot_wave, GRID, 1)
        slots[t, 0] = jnp.where(first, slot_wave, turned)
        slots[t, 1] = jnp.where(first, turned, slot_wave)
        return carry

    fetch_cond.wait()
    lax.fori_loop(0, GRID // 4, widen, 0, unroll=2)

    def transform(chunk, member):
        pair = 2 * chunk + member
        fetch_val[pair].wait()
        tb, ta, tc = table_b[...], table_a[...], table_c[...]

        def along_b(t, carry):
            rows = pl.ds(t * 4, 4)
            one = val[pair, 0, rows].reshape(block, LANES).astype(jnp.float32)
            two = val[pair, 1, rows].reshape(block, LANES).astype(jnp.float32)
            one_t = pltpu.roll(one, GRID, 1)
            two_t = pltpu.roll(two, GRID, 1)
            slot_re, slot_im = slots[t, 0], slots[t, 1]
            val_re = jnp.where(first, one, two_t)
            val_im = jnp.where(first, one_t, two)
            dens_re = val_re * slot_re + val_im * slot_im
            dens_im = val_re * slot_im - val_im * slot_re
            high, low = halves(jnp.concatenate([dens_re, dens_im], 1))
            both = three(dot_nn, tb, high, low)
            to = pl.ds(pl.multiple_of(t * 16, 16), 16)
            for sign, value in enumerate(signs(both, 4 * MAGS)):
                high, low = halves(value)
                for group in range(MAGS // 4):
                    zh[sign * 5 + group, to, :] = high[group * 16 : group * 16 + 16]
                    zl[sign * 5 + group, to, :] = low[group * 16 : group * 16 + 16]
            return carry

        lax.fori_loop(0, GRID // 4, along_b, 0, unroll=4)

        def along_a(group, carry):
            to = pl.ds(pl.multiple_of(group * 80, 16), 80)
            for sign_b in range(2):
                both = three(dot_nn, ta, zh[sign_b * 5 + group], zl[sign_b * 5 + group])
                for sign_a, value in enumerate(signs(both, 4 * MAGS)):
                    high, low = halves(value)
                    uh[sign_a * 2 + sign_b, to, :] = high
                    ul[sign_a * 2 + sign_b, to, :] = low
            return carry

        lax.fori_loop(0, MAGS // 4, along_a, 0, unroll=True)

        def along_c(quarter, carry):
            value = three(dot_nt, tc, uh[quarter], ul[quarter])
            value = value.reshape(MAGS, 8, CELLS)
            to = pl.multiple_of(quarter * 16 + member * 8, 8)
            sums[:, pl.ds(to, 8), :CELLS] = value
            sums[:, pl.ds(to + 64, 8), :CELLS] = value
            return carry

        lax.fori_loop(0, 4, along_c, 0, unroll=True)

    lane = lax.broadcasted_iota(jnp.int32, (1, LANES), 1)

    def collect(chunk):
        def upturn(mag, carry):
            value = jnp.transpose(sums[mag], (1, 0))
            cells[pl.ds(pl.multiple_of(mag * CELLS, 8), CELLS), :] = value[:CELLS]
            return carry

        lax.fori_loop(0, MAGS, upturn, 0, unroll=2)

        def gather(index, count):
            def rows(i, carry):
                for k in range(64):
                    at = i * 128 + 2 * k
                    even = cells[pl.ds(index[at], 1), :]
                    odd = cells[pl.ds(index[at + 1], 1), :]
                    picked[pl.ds(i * 64 + k, 1), :] = jnp.where(lane < 64, even, odd)
                return carry

            lax.fori_loop(0, count // 64, rows, 0)

        gather(index_p, plain.shape[1] * plain.shape[2])
        plain[chunk] = picked[...].astype(jnp.bfloat16).reshape(plain.shape[1:])
        count = weighted.shape[1] * weighted.shape[2]
        gather(index_w, count)
        band = (lane >> 3) % 2 * 2 + (lane >> 2) % 2
        gap = jnp.zeros((1, LANES), jnp.float32)
        energy = cond_energy[owner[0]]
        for v in range(4):
            gap = jnp.where(band == v, energy - val_energy[4 * chunk + v], gap)
        weight = -2.0 / (math.sqrt(8 * LANES) * gap)
        weighted[chunk] = (picked[:count] * weight).astype(jnp.bfloat16).reshape(weighted.shape[1:])

    def push(src, dst, send, recv, device):
        return pltpu.make_async_remote_copy(
            src_ref=src, dst_ref=dst, send_sem=send, recv_sem=recv, device_id=device, device_id_type=mesh
        )

    sent = []
    row_copies, col_copies, own_copies = {}, {}, {}

    def swap(chunk):
        copies = []
        for i in range(1, ROWS):
            to, at = lax.rem(row + i, ROWS), chunk * ROWS + i
            copy = push(
                weighted.at[chunk].at[to], slabs_w.at[chunk].at[row], row_send.at[at], row_recv.at[at], (to, col)
            )
            copy.start()
            copies.append(copy)
        row_copies[chunk] = copies
        copies = []
        for i in range(1, COLS):
            to, at = lax.rem(col + i, COLS), chunk * COLS + i
            copy = push(
                plain.at[chunk].at[to], slabs.at[chunk].at[slot], col_send.at[at], col_recv.at[at], (row, to)
            )
            copy.start()
            copies.append(copy)
        col_copies[chunk] = copies
        own_p = pltpu.make_async_copy(plain.at[chunk].at[col], slabs.at[chunk].at[slot], own_sem.at[2 * chunk])
        own_w = pltpu.make_async_copy(
            weighted.at[chunk].at[row], slabs_w.at[chunk].at[row], own_sem.at[2 * chunk + 1]
        )
        own_p.start()
        own_w.start()
        own_copies[chunk] = own_p, own_w
        sent.extend(row_copies[chunk] + col_copies[chunk])

    beside, spread, twin = {}, {}, {}

    def place_left(chunk):
        own_copies[chunk][1].wait()
        for copy in row_copies[chunk]:
            copy.wait_recv()
        value = placed(
            points_w[...], codes_w[row], [slabs_w[chunk, i] for i in range(ROWS)], fold_w[...]
        )
        lefts[chunk, slot] = jnp.transpose(value, (1, 0))[:64].astype(jnp.bfloat16)
        mine = lefts.at[chunk].at[slot]
        beside[chunk] = push(
            mine, mine, left_send.at[chunk * 5], left_recv.at[chunk * 5],
            (row, (x * 2 + 1 - y_lo) * 2 + core),
        )
        beside[chunk].start()
        sent.append(beside[chunk])

    def spread_left(chunk):
        beside[chunk].wait_recv()
        spread[chunk] = []
        two = lefts.at[chunk].at[pl.ds(core * 8 + x * 2, 2)]
        for i in range(1, 4):
            to, at = lax.rem(x + i, 4), chunk * 5 + i
            copy = push(two, two, left_send.at[at], left_recv.at[at], (row, (to * 2 + y_lo) * 2 + core))
            copy.start()
            spread[chunk].append(copy)
        sent.extend(spread[chunk])

    def twin_left(chunk):
        for copy in spread[chunk]:
            copy.wait_recv()
        octet, at = lefts.at[chunk].at[pl.ds(core * 8, 8)], chunk * 5 + 4
        twin[chunk] = push(octet, octet, left_send.at[at], left_recv.at[at], (row, col + 1 - 2 * core))
        twin[chunk].start()
        sent.append(twin[chunk])

    def build_left(chunk):
        twin[chunk].wait_recv()
        lefts_wide[...] = lefts[chunk].astype(jnp.float32)
        for source in range(ROWS):
            value = lefts_wide[:, source * 8 : source * 8 + 8, :].reshape(LANES, G_ROW)
            value = jnp.transpose(value, (1, 0)).astype(jnp.bfloat16)
            lanes = slice(source * LANES, (source + 1) * LANES)
            left[chunk, :G_ROW, lanes] = value
            left[chunk, G_ROW:, lanes] = dot_nn(value, turn[...]).astype(jnp.bfloat16)

    moves = {}

    def move(chunk, tile, kind, source, device, half=None):
        if half is None:
            rows = pl.ds(tile * TILE, TILE)
        else:
            rows = pl.ds(tile * TILE + half * (TILE // 2), TILE // 2)
        part = panels.at[chunk].at[source].at[rows]
        at = (chunk * TILES + tile) * KINDS + kind
        copy = push(part, part, move_send.at[at], move_recv.at[at], device)
        copy.start()
        moves[chunk, tile, kind] = copy
        sent.append(copy)

    starts, span = windows(G_COL, COLS, TILE)

    def place(chunk):
        own_copies[chunk][0].wait()
        for copy in col_copies[chunk]:
            copy.wait_recv()
        for tile in range(TILES):
            window = slice(starts[tile], starts[tile] + span)
            value = placed(
                points_p[tile * TILE : (tile + 1) * TILE], codes_p[col][:, window],
                [slabs[chunk, i, window] for i in range(COLS)], fold_p[...],
            )
            panels[chunk, row, tile * TILE : (tile + 1) * TILE, :] = value.astype(jnp.bfloat16)
            move(chunk, tile, 0, row, across)
            move(chunk, tile, 1, row, above)
            move(chunk, tile, 2, row, below)

    y_first, z_first = range(3), range(3, TILES)

    def pass_on(chunk, tile, y, kinds):
        moves[chunk, tile, kinds[0]].wait_recv()
        move(chunk, tile, kinds[2], down * 2 + y, above, 0)
        moves[chunk, tile, kinds[1]].wait_recv()
        move(chunk, tile, kinds[3], up * 2 + y, below, 1)

    def wave_one(chunk):
        for tile in y_first:
            moves[chunk, tile, 0].wait_recv()
            move(chunk, tile, 5, across_row, above)
            move(chunk, tile, 6, across_row, below)
            pass_on(chunk, tile, y_hi, (1, 2, 3, 4))

    def wave_two(chunk):
        for tile in z_first:
            pass_on(chunk, tile, y_hi, (1, 2, 3, 4))
            move(chunk, tile, 5, down * 2 + y_hi, across)
            move(chunk, tile, 6, up * 2 + y_hi, across)
        for tile in y_first:
            pass_on(chunk, tile, 1 - y_hi, (5, 6, 7, 8))

    def wave_three(chunk):
        for tile in z_first:
            moves[chunk, tile, 3].wait_recv()
            move(chunk, tile, 7, far * 2 + y_hi, across, 0)
            moves[chunk, tile, 4].wait_recv()
            move(chunk, tile, 8, far * 2 + y_hi, across, 1)

    outs = []

    def multiply(chunk, tile):
        for kind in (3, 4, 7, 8) if tile in y_first else (0, 5, 6, 7, 8):
            moves[chunk, tile, kind].wait_recv()
        rows = slice(tile * TILE, (tile + 1) * TILE)
        right = jnp.concatenate([panels[chunk, source, rows, :] for source in range(ROWS)], 1)
        value = dot_nt(left[chunk], right).reshape(2, G_ROW, TILE)
        if chunk == 0:
            totals[tile] = value
            return
        totals[tile] = totals[tile] + value
        copy = pltpu.make_async_copy(
            totals.at[tile], out.at[:, :, pl.ds(tile * TILE, TILE)], out_sem.at[tile]
        )
        copy.start()
        outs.append(copy)

    transform(0, 0)
    transform(0, 1)
    collect(0)
    pl.semaphore_wait(barrier, COLS + ROWS - 2)
    swap(0)
    transform(1, 0)
    place_left(0)
    place(0)
    transform(1, 1)
    wave_one(0)
    spread_left(0)
    collect(1)
    swap(1)
    wave_two(0)
    twin_left(0)
    place_left(1)
    place(1)
    wave_three(0)
    spread_left(1)
    wave_one(1)
    build_left(0)
    for tile in range(3):
        multiply(0, tile)
    twin_left(1)
    wave_two(1)
    for tile in range(3, TILES):
        multiply(0, tile)
    wave_three(1)
    build_left(1)
    for tile in range(TILES):
        multiply(1, tile)
    for copy in sent:
        copy.wait_send()
    for copy in outs:
        copy.wait()


def on_device(val_wave, cond_wave, val_energy, cond_energy, band_owner, grid_map):
    index_p, codes_p, _ = orbit_lists(G_COL, COLS)
    index_w, codes_w, _ = orbit_lists(G_ROW, ROWS)
    codes_p, codes_w = paired(codes_p), paired(codes_w)
    rows_p, rows_w = codes_p.shape[2], codes_w.shape[2]
    constants = [
        codes_p, codes_w, *dft_tables(),
        fold_table(COLS, LANES), fold_table(ROWS, LANES), turn_table(),
    ]
    smem = pl.BlockSpec(memory_space=pltpu.SMEM)
    vmem = pl.BlockSpec(memory_space=pltpu.VMEM)
    hbm = pl.BlockSpec(memory_space=pl.ANY)
    dma = pltpu.SemaphoreType.DMA
    bf16, f32 = jnp.bfloat16, jnp.float32
    return pl.pallas_call(
        whole_kernel,
        in_specs=[smem] * 5 + [vmem] * (1 + len(constants)) + [hbm] * 2,
        out_specs=hbm,
        out_shape=jax.ShapeDtypeStruct((2, G_ROW, G_COL), f32),
        scratch_shapes=[
            pltpu.VMEM((4, 2, GRID, GRID, LANES), bf16),
            pltpu.VMEM((1, GRID, GRID, LANES), bf16),
            pltpu.VMEM((GRID // 4, 2, 4 * GRID, LANES), f32),
            pltpu.VMEM((10, 4 * GRID, 2 * LANES), bf16),
            pltpu.VMEM((10, 4 * GRID, 2 * LANES), bf16),
            pltpu.VMEM((4, CELLS, 2 * LANES), bf16),
            pltpu.VMEM((4, CELLS, 2 * LANES), bf16),
            pltpu.VMEM((MAGS, LANES, 512), f32),
            pltpu.VMEM((MAGS * CELLS, LANES), f32),
            pltpu.VMEM((COLS * rows_p, LANES), f32),
            pltpu.VMEM((G_COL, 1), jnp.int32),
            pltpu.VMEM((G_ROW, 1), jnp.int32),
            pltpu.VMEM((LANES, LANES), f32),
            pltpu.VMEM((2, COLS, rows_p, LANES), bf16),
            pltpu.VMEM((2, ROWS, rows_w, LANES), bf16),
            pltpu.VMEM((2, COLS, rows_p, LANES), bf16),
            pltpu.VMEM((2, ROWS, rows_w, LANES), bf16),
            pltpu.VMEM((2, COLS, 64, G_ROW), bf16),
            pltpu.VMEM((COLS, 64, G_ROW), f32),
            pltpu.VMEM((2, 2 * G_ROW, ROWS * LANES), bf16),
            pltpu.VMEM((2, ROWS, G_COL, LANES), bf16),
            pltpu.VMEM((TILES, 2, G_ROW, TILE), f32),
            dma((4,)), dma, dma((4,)), dma((TILES,)),
            dma((2 * COLS,)), dma((2 * COLS,)), dma((2 * ROWS,)), dma((2 * ROWS,)), dma((10,)), dma((10,)),
            dma((2 * TILES * KINDS,)), dma((2 * TILES * KINDS,)),
        ],
        compiler_params=pltpu.CompilerParams(
            collective_id=0, has_side_effects=True, vmem_limit_bytes=62 * 2**20
        ),
        name="whole",
    )(
        band_owner, cond_energy, val_energy, jnp.asarray(index_p.ravel()), jnp.asarray(index_w.ravel()),
        grid_map.reshape(NG // LANES, LANES), *(jnp.asarray(value) for value in constants),
        val_wave, cond_wave,
    )


def solution(mesh):
    in_specs = (P(), P(("row", "col"), None, None, None), P(), P(), P(("row", "col")), P())
    out_specs = P(None, "row", "col")
    return jax.shard_map(
        on_device, mesh=mesh, in_specs=in_specs, out_specs=out_specs, check_vma=False
    )
```

profile of v0, /device:TPU:1, one launch (start us, length us, event | category | flops | bytes accessed | tf_op | source)
XLA Modules:
  0.0 108.8 jit_solution(3371686199232902559)
XLA Ops:
  0.7 103.8 %whole.1 = f32[2,256,1920]{2,1,0:T(8,128)} custom-call(s32[1]{0:T(128)S(6)} %copy.18.owner, f32[128]{0:T(128)} %cond_energy.1, f32[8]{0:T(128)} %val_energy.1, s32[5120]{0:T(1024)} %constant.20.clone.index_p, s32[512]{0:T(512)} %constant.21.clone.index_w, s32[240,128]{1,0:T(8,128)} %bitcast.1, s32[16,2,160]{2,1,0:T(2,128)} %constant.22.clone.codes_p, ...), custom_call_target="tpu_custom_call" | custom-call | tf_op jit(solution)/shard_map/whole/pallas_call | solution.py:534
  104.5 4.3 %copy.19 = f32[2,256,1920]{2,1,0:T(8,128)} copy(f32[2,256,1920]{2,1,0:T(8,128)} %whole.1) | data formatting | bytes 7864320
where the time goes:
time: 109 us
  Pallas kernels  104 us (95%)
  local copies, waits for them, and re-layouts  4.3 us (4%)
    pallas_call x1, Pallas kernels, on_device(): pl.pallas_call(whole_kernel, in_specs=[smem] * 5 + [vmem] * (1 + len(cons...  104 us
    unnamed x1, local copies, waits for them, and re-layouts  4.3 us

commit v1 on v0

--- a/solution.py
+++ b/solution.py
@@ -235,10 +235,10 @@
     fetch_cond.wait()
     lax.fori_loop(0, GRID // 4, widen, 0, unroll=2)
 
-    def transform(chunk, member):
+    def transform_b(chunk, member):
         pair = 2 * chunk + member
         fetch_val[pair].wait()
-        tb, ta, tc = table_b[...], table_a[...], table_c[...]
+        tb = table_b[...]
 
         def along_b(t, carry):
             rows = pl.ds(t * 4, 4)
@@ -261,7 +261,10 @@
                     zl[sign * 5 + group, to, :] = low[group * 16 : group * 16 + 16]
             return carry
 
-        lax.fori_loop(0, GRID // 4, along_b, 0, unroll=4)
+        lax.fori_loop(0, GRID // 4, along_b, 0, unroll=8)
+
+    def transform_ac(member):
+        ta, tc = table_a[...], table_c[...]
 
         def along_a(group, carry):
             to = pl.ds(pl.multiple_of(group * 80, 16), 80)
@@ -287,7 +290,7 @@
 
     lane = lax.broadcasted_iota(jnp.int32, (1, LANES), 1)
 
-    def collect(chunk):
+    def collect():
         def upturn(mag, carry):
             value = jnp.transpose(sums[mag], (1, 0))
             cells[pl.ds(pl.multiple_of(mag * CELLS, 8), CELLS), :] = value[:CELLS]
@@ -295,21 +298,43 @@
 
         lax.fori_loop(0, MAGS, upturn, 0, unroll=2)
 
-        def gather(index, count):
-            def rows(i, carry):
-                for k in range(64):
-                    at = i * 128 + 2 * k
-                    even = cells[pl.ds(index[at], 1), :]
-                    odd = cells[pl.ds(index[at + 1], 1), :]
-                    picked[pl.ds(i * 64 + k, 1), :] = jnp.where(lane < 64, even, odd)
-                return carry
-
-            lax.fori_loop(0, count // 64, rows, 0)
-
-        gather(index_p, plain.shape[1] * plain.shape[2])
-        plain[chunk] = picked[...].astype(jnp.bfloat16).reshape(plain.shape[1:])
+    def gather(index, base, to, count):
+        def rows(i, carry):
+            for k in range(32):
+                at = base + i * 64 + 2 * k
+                even = cells[pl.ds(index[at], 1), :]
+                odd = cells[pl.ds(index[at + 1], 1), :]
+                picked[pl.ds(to + i * 32 + k, 1), :] = jnp.where(lane < 64, even, odd)
+            return carry
+
+        lax.fori_loop(0, count // 32, rows, 0)
+
+    def push(src, dst, send, recv, device):
+        return pltpu.make_async_remote_copy(
+            src_ref=src, dst_ref=dst, send_sem=send, recv_sem=recv, device_id=device, device_id_type=mesh
+        )
+
+    sent = []
+    row_copies, col_copies, own_copies = {}, {}, {}
+
+    def swap(chunk):
+        rows = plain.shape[2]
+        copies = []
+        for i in list(range(1, COLS)) + [0]:
+            to, at = lax.rem(col + i, COLS), chunk * COLS + i
+            gather(index_p, to * (2 * rows), i * rows, rows)
+            plain[chunk, to] = picked[i * rows : (i + 1) * rows].astype(jnp.bfloat16)
+            src, dst = plain.at[chunk].at[to], slabs.at[chunk].at[slot]
+            if i == 0:
+                own_p = pltpu.make_async_copy(src, dst, own_sem.at[2 * chunk])
+                own_p.start()
+            else:
+                copy = push(src, dst, col_send.at[at], col_recv.at[at], (row, to))
+                copy.start()
+                copies.append(copy)
+        col_copies[chunk] = copies
         count = weighted.shape[1] * weighted.shape[2]
-        gather(index_w, count)
+        gather(index_w, 0, 0, count)
         band = (lane >> 3) % 2 * 2 + (lane >> 2) % 2
         gap = jnp.zeros((1, LANES), jnp.float32)
         energy = cond_energy[owner[0]]
@@ -317,16 +342,6 @@
             gap = jnp.where(band == v, energy - val_energy[4 * chunk + v], gap)
         weight = -2.0 / (math.sqrt(8 * LANES) * gap)
         weighted[chunk] = (picked[:count] * weight).astype(jnp.bfloat16).reshape(weighted.shape[1:])
-
-    def push(src, dst, send, recv, device):
-        return pltpu.make_async_remote_copy(
-            src_ref=src, dst_ref=dst, send_sem=send, recv_sem=recv, device_id=device, device_id_type=mesh
-        )
-
-    sent = []
-    row_copies, col_copies, own_copies = {}, {}, {}
-
-    def swap(chunk):
         copies = []
         for i in range(1, ROWS):
             to, at = lax.rem(row + i, ROWS), chunk * ROWS + i
@@ -336,20 +351,9 @@
             copy.start()
             copies.append(copy)
         row_copies[chunk] = copies
-        copies = []
-        for i in range(1, COLS):
-            to, at = lax.rem(col + i, COLS), chunk * COLS + i
-            copy = push(
-                plain.at[chunk].at[to], slabs.at[chunk].at[slot], col_send.at[at], col_recv.at[at], (row, to)
-            )
-            copy.start()
-            copies.append(copy)
-        col_copies[chunk] = copies
-        own_p = pltpu.make_async_copy(plain.at[chunk].at[col], slabs.at[chunk].at[slot], own_sem.at[2 * chunk])
         own_w = pltpu.make_async_copy(
             weighted.at[chunk].at[row], slabs_w.at[chunk].at[row], own_sem.at[2 * chunk + 1]
         )
-        own_p.start()
         own_w.start()
         own_copies[chunk] = own_p, own_w
         sent.extend(row_copies[chunk] + col_copies[chunk])
@@ -480,31 +484,34 @@
         copy.start()
         outs.append(copy)
 
-    transform(0, 0)
-    transform(0, 1)
-    collect(0)
+    for member in range(2):
+        transform_b(0, member)
+        transform_ac(member)
+    collect()
     pl.semaphore_wait(barrier, COLS + ROWS - 2)
     swap(0)
-    transform(1, 0)
+    transform_b(1, 0)
+    transform_ac(0)
+    transform_b(1, 1)
+    place(0)
+    transform_ac(1)
+    collect()
+    swap(1)
+    wave_one(0)
     place_left(0)
-    place(0)
-    transform(1, 1)
-    wave_one(0)
+    wave_two(0)
     spread_left(0)
-    collect(1)
-    swap(1)
-    wave_two(0)
+    place(1)
+    wave_three(0)
     twin_left(0)
     place_left(1)
-    place(1)
-    wave_three(0)
-    spread_left(1)
     wave_one(1)
     build_left(0)
     for tile in range(3):
         multiply(0, tile)
+    spread_left(1)
+    wave_two(1)
     twin_left(1)
-    wave_two(1)
     for tile in range(3, TILES):
         multiply(0, tile)
     wave_three(1)

time: 109 us -> 103 us (0.945)
  Pallas kernels: 104 us -> 97.5 us
    pallas_call x1, Pallas kernels: 104 us -> 97.5 us  [on_device(): pl.pallas_call(whole_kernel, in_specs=[smem] * 5 + [vmem] * (1 + len(cons...]
where the time goes in v1:
time: 103 us; the launch traced here: 102 us
  Pallas kernels  97.5 us (95%)
  local copies, waits for them, and re-layouts  4.3 us (4%)
    pallas_call x1, Pallas kernels, on_device(): pl.pallas_call(whole_kernel, in_specs=[smem] * 5 + [vmem] * (1 + len(cons...  97.5 us
    unnamed x1, local copies, waits for them, and re-layouts  4.3 us

profile of v1, /device:TPU:1, one launch (start us, length us, event | category | flops | bytes accessed | tf_op | source)
XLA Modules:
  0.0 102.5 jit_solution(12438733333029009019)
XLA Ops:
  0.7 97.5 %whole.1 = f32[2,256,1920]{2,1,0:T(8,128)} custom-call(s32[1]{0:T(128)S(6)} %copy.18.owner, f32[128]{0:T(128)} %cond_energy.1, f32[8]{0:T(128)} %val_energy.1, s32[5120]{0:T(1024)} %constant.20.clone.index_p, s32[512]{0:T(512)} %constant.21.clone.index_w, s32[240,128]{1,0:T(8,128)} %bitcast.1, s32[16,2,160]{2,1,0:T(2,128)} %constant.22.clone.codes_p, ...), custom_call_target="tpu_custom_call" | custom-call | tf_op jit(solution)/shard_map/whole/pallas_call | solution.py:541
  98.2 4.3 %copy.19 = f32[2,256,1920]{2,1,0:T(8,128)} copy(f32[2,256,1920]{2,1,0:T(8,128)} %whole.1) | data formatting | bytes 7864320
